TPU v7x, 32 devices: a whole 2x2x4 slice. The times are simulated.
32 devices in a mesh: bins: 8 (over z, core), diag: 4 (over y, x).
Axes of the slice: x: 2, y: 2, z: 4, core: 2. Of those that a mesh axis runs over, the one named last changes fastest.
Arguments:
- embeddings: bfloat16 [1024, 512], P('bins'), may hold values from -6 to 6
- w_row: bfloat16 [512, 32], replicated, may hold values from -0.25 to 0.25
- w_col: bfloat16 [512, 32], replicated, may hold values from -0.25 to 0.25
- conv_w: bfloat16 [2, 9, 32, 32], replicated, may hold values from -0.375 to 0.375
- coef: float32 [2, 8, 32], replicated, may hold values from 0.5 to 2
- w_out: float32 [32], replicated, may hold values from -1 to 1
- dilation: int32 [2], replicated, may hold values from 1 to 32, as said below
- band_tiles: int32 [8], replicated, may hold values from 1 to 4
- bucket: int32 [4], replicated, may hold values from 0 to 7
- target: float32 [1024, 512], P('bins', 'diag'), may hold values from -6 to 6
Outputs:
- loss: float32 [1], replicated
- grad_embeddings: float32 [1024, 512], P('bins')
- grad_conv: float32 [2, 9, 32, 32], replicated
- grad_coef: float32 [2, 8, 32], replicated
- grad_out: float32 [32], replicated
- grad_row: float32 [512, 32], replicated
- grad_col: float32 [512, 32], replicated
Inputs may be any that keep to these rules, and one draw needn't show every extreme that they name: Each entry is a power of two; some layer has dilation 32.
All inputs are finite; a program needn't handle non-finite values.
Results may differ from a plain program's by a relative error of at most 0.011.
Values may be sent and summed in bfloat16 or wider, within the bound.
A program may use at most 64 MiB of HBM per device.

v0:
```python
import jax
import jax.numpy as jnp
from jax import lax
from jax.experimental import pallas as pl
from jax.experimental.pallas import tpu as pltpu
from jax.sharding import PartitionSpec as P

MAPS = 32
TILE = 128
LAYERS = 2
REACH = 32
BUCKETS = 8


MESH = pl.DeviceIdType.MESH


def reduce_kernel(nb, nd, x_ref, o_ref, buf_a, acc_a, buf_b, acc_b, *sems):
    sa, ra, sb, rb, sc, rc, sd, rd = sems
    b = lax.axis_index("bins")
    g = lax.axis_index("diag")
    rows_a = x_ref.shape[0] // nd
    rows_b = rows_a // nb
    peers_g = [lax.rem(g + k, nd) for k in range(nd)]
    peers_b = [lax.rem(b + k, nb) for k in range(nb)]
    barrier = pltpu.get_barrier_semaphore()
    for k in range(1, nd):
        pl.semaphore_signal(barrier, inc=1, device_id=(b, peers_g[k]), device_id_type=MESH)
    for k in range(1, nb):
        pl.semaphore_signal(barrier, inc=1, device_id=(peers_b[k], g), device_id_type=MESH)
    pl.semaphore_wait(barrier, nd + nb - 2)

    def rows_of(index, count):
        return pl.ds(pl.multiple_of(index * count, 8), count)

    def send(src, dst, ssem, rsem, target):
        copy = pltpu.make_async_remote_copy(
            src_ref=src,
            dst_ref=dst,
            send_sem=ssem,
            recv_sem=rsem,
            device_id=target,
            device_id_type=MESH,
        )
        copy.start()
        return copy

    copies = [
        send(
            x_ref.at[rows_of(peers_g[k], rows_a)],
            buf_a.at[k],
            sa.at[k],
            ra.at[k],
            (b, peers_g[k]),
        )
        for k in range(1, nd)
    ]
    total = x_ref[rows_of(g, rows_a), :]
    for k in range(1, nd):
        copies[k - 1].wait()
        total = total + buf_a[k]
    acc_a[...] = total
    copies = [
        send(
            acc_a.at[rows_of(peers_b[k], rows_b)],
            buf_b.at[k],
            sb.at[k],
            rb.at[k],
            (peers_b[k], g),
        )
        for k in range(1, nb)
    ]
    total = acc_a[rows_of(b, rows_b), :]
    for k in range(1, nb):
        copies[k - 1].wait()
        total = total + buf_b[k]
    acc_b[rows_of(b, rows_b), :] = total
    mine = acc_b.at[rows_of(b, rows_b)]
    copies = [
        send(mine, mine, sc.at[k], rc.at[k], (peers_b[k], g)) for k in range(1, nb)
    ]
    for copy in copies:
        copy.wait()
    o_ref[rows_of(g, rows_a), :] = acc_b[...]
    place = o_ref.at[rows_of(g, rows_a)]
    copies = [
        send(acc_b, place, sd.at[k], rd.at[k], (b, peers_g[k])) for k in range(1, nd)
    ]
    for copy in copies:
        copy.wait()


def all_sum(flat, ident):
    nb, nd = lax.axis_size("bins"), lax.axis_size("diag")
    unit = nb * nd * 8
    rows = -(-flat.shape[0] // (128 * unit)) * unit
    x = jnp.pad(flat, (0, rows * 128 - flat.shape[0])).reshape(rows, 128)
    rows_a, rows_b = rows // nd, rows // nd // nb
    dma = pltpu.SemaphoreType.DMA
    out = pl.pallas_call(
        lambda *refs: reduce_kernel(nb, nd, *refs),
        out_shape=jax.ShapeDtypeStruct((rows, 128), jnp.float32),
        in_specs=[pl.BlockSpec(memory_space=pltpu.VMEM)],
        out_specs=pl.BlockSpec(memory_space=pltpu.VMEM),
        scratch_shapes=[
            pltpu.VMEM((nd, rows_a, 128), jnp.float32),
            pltpu.VMEM((rows_a, 128), jnp.float32),
            pltpu.VMEM((nb, rows_b, 128), jnp.float32),
            pltpu.VMEM((rows_a, 128), jnp.float32),
            dma((nd,)),
            dma((nd,)),
            dma((nb,)),
            dma((nb,)),
            dma((nb,)),
            dma((nb,)),
            dma((nd,)),
            dma((nd,)),
        ],
        compiler_params=pltpu.CompilerParams(
            collective_id=ident, has_side_effects=True, vmem_limit_bytes=16 * 2**20
        ),
    )(x)
    return out.reshape(-1)[: flat.shape[0]]


DIRS = [(-1, 0), (1, 0), (0, -1), (0, 1), (-1, -1), (-1, 1), (1, -1), (1, 1)]
BLOCKS = 4
SUB = 32
LANES = BLOCKS * MAPS
FACE = SUB * 32
CORNER = SUB * 8


def gate_of(v):
    return 1.0 / (1.0 + jnp.exp(-v))


def rounded(v):
    return v.astype(jnp.bfloat16).astype(jnp.float32)


def lane_group(shape):
    return lax.broadcasted_iota(jnp.int32, shape, len(shape) - 1) // MAPS


def packed(cells, group):
    piece = cells.shape[1] // BLOCKS
    total = None
    for q in range(BLOCKS):
        part = cells[:, q * piece : (q + 1) * piece, :].reshape(-1, LANES)
        turn = (MAPS * (q - group)) % LANES
        part = pltpu.roll(part, turn, 1) if turn else part
        total = part if total is None else jnp.where(lane_group(part.shape) == q, part, total)
    return total


def unpacked(part, group):
    pieces = []
    for q in range(BLOCKS):
        turn = (MAPS * (group - q)) % LANES
        pieces.append(pltpu.roll(part, turn, 1) if turn else part)
    return pieces


def step_kernel(
    nb,
    nd,
    dil_ref,
    lim_ref,
    colm_ref,
    cols_ref,
    rowm_ref,
    rows_ref,
    wf_ref,
    wb_ref,
    par_ref,
    target_ref,
    kern_ref,
    stat_ref,
    rowg_ref,
    colg_ref,
    ext,
    sh0,
    sh1,
    sh2,
    cur,
    mask_buf,
    mixed_buf,
    adj_buf,
    gm_buf,
    send_face,
    send_corner,
    recv_face,
    recv_corner,
    corner_f,
    send_sem,
    recv_sem,
):
    b = lax.axis_index("bins")
    g = lax.axis_index("diag")
    row_start = b * TILE
    col_start = g * TILE

    def there(sx, sg):
        x, y = b + sx, g + sg
        return (x >= 0) & (x < nb) & (y >= 0) & (y < nd)

    def place(sx, sg):
        return (lax.rem(b + sx + nb, nb), lax.rem(g + sg + nd, nd))

    for n, (sx, sg) in enumerate(DIRS):

        @pl.when(jnp.logical_not(there(-sx, -sg)))
        def _():
            for e in range(3):
                if n < 4:
                    recv_face[e, n] = jnp.zeros((FACE, LANES), jnp.bfloat16)
                else:
                    recv_corner[e, n - 4] = jnp.zeros((CORNER, LANES), jnp.bfloat16)

    barrier = pltpu.get_barrier_semaphore()
    for sx, sg in DIRS:

        @pl.when(there(sx, sg))
        def _():
            pl.semaphore_signal(barrier, inc=1, device_id=place(sx, sg), device_id_type=MESH)

    pl.semaphore_wait(barrier, sum(there(sx, sg).astype(jnp.int32) for sx, sg in DIRS))

    def copy_of(e, n):
        if n < 4:
            src, dst = send_face.at[n], recv_face.at[e, n]
        else:
            src, dst = send_corner.at[n - 4], recv_corner.at[e, n - 4]
        return pltpu.make_async_remote_copy(
            src_ref=src,
            dst_ref=dst,
            send_sem=send_sem.at[e, n],
            recv_sem=recv_sem.at[e, n],
            device_id=place(*DIRS[n]),
            device_id_type=MESH,
        )

    def exchange_start(e):
        for n in (2, 3, 0, 1, 4, 5, 6, 7):
            sx, sg = DIRS[n]
            lo = 0 if sg < 0 else TILE - 32
            if n < 2:
                value = packed(cur[...], 0 if sx < 0 else BLOCKS - 1)
                send_face[n] = value.astype(jnp.bfloat16)
            elif n < 4:
                value = cur[:, lo : lo + 32, :].reshape(FACE, LANES)
                send_face[n] = value.astype(jnp.bfloat16)
            else:
                value = packed(cur[:, lo : lo + 32, :], 0 if sx < 0 else BLOCKS - 1)
                send_corner[n - 4] = value.astype(jnp.bfloat16)

            @pl.when(there(sx, sg))
            def _():
                copy_of(e, n).start()

    def exchange_end(e):
        for n, (sx, sg) in enumerate(DIRS):

            @pl.when(there(-sx, -sg))
            def _():
                copy_of(e, n).wait_recv()

            @pl.when(there(sx, sg))
            def _():
                copy_of(e, n).wait_send()

        for c in range(4):
            corner_f[c] = recv_corner[e, c].astype(jnp.float32)

        def fill(xi, carry):
            face_rows = pl.ds(pl.multiple_of(xi * 32, 32), 32)
            corner_rows = pl.ds(pl.multiple_of(xi * 8, 8), 8)

            def face(n):
                return recv_face[e, n, face_rows, :].astype(jnp.float32)

            def corner(n):
                return corner_f[n - 4, corner_rows, :]

            mid = jnp.concatenate([face(3), cur[xi], face(2)], axis=0)
            low = jnp.concatenate(
                unpacked(corner(7), 0) + unpacked(face(1), 0) + unpacked(corner(6), 0), axis=0
            )
            high = jnp.concatenate(
                unpacked(corner(5), 3) + unpacked(face(0), 3) + unpacked(corner(4), 3), axis=0
            )
            store_ext(xi, mid, low, high)
            return carry

        lax.fori_loop(0, SUB, fill, 0)

    def store_ext(xi, mid, low, high):
        group = lane_group(mid.shape)
        ext[SUB + xi] = mid
        ext[xi] = jnp.where(group == 0, low, pltpu.roll(mid, MAPS, 1))
        ext[2 * SUB + xi] = jnp.where(group == BLOCKS - 1, high, pltpu.roll(mid, LANES - MAPS, 1))

    def shift(sh, d):
        def body(xi, carry):
            for j in range(3):
                window = ext[xi, pl.ds(REACH + (j - 1) * d, TILE), :]
                sh[xi, :, j * LANES : (j + 1) * LANES] = window.astype(jnp.bfloat16)
            return carry

        lax.fori_loop(0, 3 * SUB, body, 0)

    def windows(sh, c, i, d):
        return sh[pl.ds(SUB + 8 * c + (i - 1) * d, 8)].reshape(8 * TILE, 3 * LANES)

    def convolved(sh, w_ref, layer, c, d):
        total = None
        for i in range(3):
            part = jnp.dot(
                windows(sh, c, i, d), w_ref[layer, i], preferred_element_type=jnp.float32
            )
            total = part if total is None else total + part
        return total

    def kernel_sums(sh, layer, d):
        for i in range(3):
            kern_ref[layer, i] = jnp.zeros((LANES, 3 * LANES), jnp.float32)

        def body(c, carry):
            left = gm_buf[rows_at(c), :]
            for i in range(3):
                kern_ref[layer, i] += lax.dot_general(
                    left,
                    windows(sh, c, i, d),
                    (((0,), (0,)), ((), ())),
                    preferred_element_type=jnp.float32,
                )
            return carry

        lax.fori_loop(0, SUB // 8, body, 0)

    def rows_at(c):
        return pl.ds(pl.multiple_of(c * 8 * TILE, 8 * TILE), 8 * TILE)

    def gather_stat(index, value):
        stat_ref[index] += jnp.sum(value.reshape(TILE, 8, LANES), axis=0)

    d0 = dil_ref[0]
    d1 = dil_ref[1]
    scale0 = par_ref[0:1, :]
    scale1 = par_ref[1:2, :]
    read = par_ref[2:3, :]
    for n in range(4):
        stat_ref[n] = jnp.zeros((8, LANES), jnp.float32)
    colg_ref[...] = jnp.zeros_like(colg_ref)

    def first(xi, carry):
        shape = (TILE + 2 * REACH, LANES)
        s = col_start - REACH + lax.broadcasted_iota(jnp.int32, shape, 0)
        group = lane_group(shape)
        window = pl.ds(SUB - 1 - xi, TILE + 2 * REACH)

        def cells(col_ref, row_ref, x, limit):
            pre = row_ref[pl.ds(xi, 1), :] + col_ref[window, :]
            inside = (s >= 0) & (s < limit) & (row_start + x - s >= 0)
            return inside, rounded(jnp.where(inside, pre * gate_of(pre), 0.0))

        inside, mid = cells(colm_ref, rowm_ref, SUB * group + xi, lim_ref[1])
        mask_buf[pl.ds(pl.multiple_of(xi * TILE, TILE), TILE), :] = inside.astype(jnp.float32)[
            REACH : REACH + TILE
        ]
        early = group < 2
        _, side = cells(
            cols_ref,
            rows_ref,
            jnp.where(early, xi - SUB, TILE + xi),
            jnp.where(early, lim_ref[0], lim_ref[2]),
        )
        store_ext(xi, mid, side, side)
        return carry

    lax.fori_loop(0, SUB, first, 0)
    shift(sh0, d0)

    def layer_first(c, carry):
        mixed = convolved(sh0, wf_ref, 0, c, d0)
        mixed_buf[rows_at(c), :] = mixed
        state = ext[pl.ds(SUB + 8 * c, 8), REACH : REACH + TILE, :].reshape(8 * TILE, LANES)
        state = mask_buf[rows_at(c), :] * (state + scale0 * (mixed * gate_of(mixed)))
        cur[pl.ds(8 * c, 8)] = rounded(state).reshape(8, TILE, LANES)
        return carry

    lax.fori_loop(0, SUB // 8, layer_first, 0)
    exchange_start(0)
    exchange_end(0)
    shift(sh1, d1)

    def layer_second(c, carry):
        mixed = convolved(sh1, wf_ref, 1, c, d1)
        gate = gate_of(mixed)
        act = mixed * gate
        mask = mask_buf[rows_at(c), :]
        state = ext[pl.ds(SUB + 8 * c, 8), REACH : REACH + TILE, :].reshape(8 * TILE, LANES)
        state = rounded(mask * (state + scale1 * act))
        terms = read * state
        high = terms.astype(jnp.bfloat16)
        low = (terms - high.astype(jnp.float32)).astype(jnp.bfloat16)
        a = lax.broadcasted_iota(jnp.int32, (LANES, LANES), 0) // MAPS
        z = lax.broadcasted_iota(jnp.int32, (LANES, LANES), 1) // MAPS
        ones = (a == z).astype(jnp.float32).astype(jnp.bfloat16)
        pred = jnp.dot(high, ones, preferred_element_type=jnp.float32) + jnp.dot(
            low, ones, preferred_element_type=jnp.float32
        )
        resid = mask * (pred - target_ref[rows_at(c), :])
        gather_stat(3, resid * resid)
        gather_stat(2, resid * state)
        adjoint = read * resid
        adj_buf[rows_at(c), :] = adjoint
        gather_stat(1, adjoint * act)
        grad = adjoint * scale1 * (gate * (1.0 + mixed * (1.0 - gate)))
        gm_buf[rows_at(c), :] = grad.astype(jnp.bfloat16)
        cur[pl.ds(8 * c, 8)] = rounded(grad).reshape(8, TILE, LANES)
        return carry

    lax.fori_loop(0, SUB // 8, layer_second, 0)
    exchange_start(1)
    kernel_sums(sh1, 1, d1)
    exchange_end(1)
    shift(sh2, d1)

    def back_second(c, carry):
        mask = mask_buf[rows_at(c), :]
        adjoint = mask * (adj_buf[rows_at(c), :] + convolved(sh2, wb_ref, 1, c, d1))
        adj_buf[rows_at(c), :] = adjoint
        mixed = mixed_buf[rows_at(c), :]
        gate = gate_of(mixed)
        gather_stat(0, adjoint * (mixed * gate))
        grad = adjoint * scale0 * (gate * (1.0 + mixed * (1.0 - gate)))
        gm_buf[rows_at(c), :] = grad.astype(jnp.bfloat16)
        cur[pl.ds(8 * c, 8)] = rounded(grad).reshape(8, TILE, LANES)
        return carry

    lax.fori_loop(0, SUB // 8, back_second, 0)
    exchange_start(2)
    kernel_sums(sh0, 0, d0)
    exchange_end(2)
    shift(sh2, d0)

    def back_first(c, carry):
        mask = mask_buf[rows_at(c), :]
        adjoint = mask * (adj_buf[rows_at(c), :] + convolved(sh2, wb_ref, 0, c, d0))
        adj_buf[rows_at(c), :] = adjoint
        return carry

    lax.fori_loop(0, SUB // 8, back_first, 0)

    def last(xi, carry):
        pre = rowm_ref[pl.ds(xi, 1), :] + colm_ref[pl.ds(SUB - 1 - xi + REACH, TILE), :]
        gate = gate_of(pre)
        grad = adj_buf[pl.ds(pl.multiple_of(xi * TILE, TILE), TILE), :]
        grad = grad * gate * (1.0 + pre * (1.0 - gate))
        rowg_ref[pl.ds(xi, 1), :] = jnp.sum(grad, axis=0, keepdims=True)
        colg_ref[pl.ds(SUB - 1 - xi, TILE), :] += grad
        return carry

    lax.fori_loop(0, SUB, last, 0)


def step_call(*args):
    nb, nd = lax.axis_size("bins"), lax.axis_size("diag")
    f32, bf16 = jnp.float32, jnp.bfloat16
    vmem = pl.BlockSpec(memory_space=pltpu.VMEM)
    smem = pl.BlockSpec(memory_space=pltpu.SMEM)
    cells = SUB * TILE
    return pl.pallas_call(
        lambda *refs: step_kernel(nb, nd, *refs),
        out_shape=(
            jax.ShapeDtypeStruct((2, 3, LANES, 3 * LANES), f32),
            jax.ShapeDtypeStruct((4, 8, LANES), f32),
            jax.ShapeDtypeStruct((SUB, LANES), f32),
            jax.ShapeDtypeStruct((SUB + TILE, LANES), f32),
        ),
        in_specs=[smem, smem] + [vmem] * 8,
        out_specs=(vmem,) * 4,
        scratch_shapes=[
            pltpu.VMEM((3 * SUB, TILE + 2 * REACH, LANES), f32),
            pltpu.VMEM((3 * SUB, TILE, 3 * LANES), bf16),
            pltpu.VMEM((3 * SUB, TILE, 3 * LANES), bf16),
            pltpu.VMEM((3 * SUB, TILE, 3 * LANES), bf16),
            pltpu.VMEM((SUB, TILE, LANES), f32),
            pltpu.VMEM((cells, LANES), f32),
            pltpu.VMEM((cells, LANES), f32),
            pltpu.VMEM((cells, LANES), f32),
            pltpu.VMEM((cells, LANES), bf16),
            pltpu.VMEM((4, FACE, LANES), bf16),
            pltpu.VMEM((4, CORNER, LANES), bf16),
            pltpu.VMEM((3, 4, FACE, LANES), bf16),
            pltpu.VMEM((3, 4, CORNER, LANES), bf16),
            pltpu.VMEM((4, CORNER, LANES), f32),
            pltpu.SemaphoreType.DMA((3, 8)),
            pltpu.SemaphoreType.DMA((3, 8)),
        ],
        compiler_params=pltpu.CompilerParams(
            collective_id=3, has_side_effects=True, vmem_limit_bytes=60 * 2**20
        ),
    )(*args)


def local(embeddings, w_row, w_col, conv_w, coef, w_out, dilation, band_tiles, bucket, target):
    rows = embeddings.shape[0]
    width = target.shape[1]
    diag_count = lax.axis_size("diag")
    total_bins = rows * lax.axis_size("bins")
    band_cols = width * diag_count
    tile_total = band_tiles.shape[0]
    zero = jnp.zeros((), jnp.int32)
    row_start = lax.axis_index("bins") * rows
    col_start = lax.axis_index("diag") * width
    device_bucket = jnp.sum(
        jnp.where(jnp.arange(diag_count, dtype=jnp.int32) == lax.axis_index("diag"), bucket, 0)
    )
    choose = (jnp.arange(BUCKETS, dtype=jnp.int32) == device_bucket).astype(jnp.float32)
    tile_ids = jnp.arange(tile_total, dtype=jnp.int32)[None, :]

    def row_limit(bins_col):
        tiles = jnp.clip(bins_col // TILE, 0, tile_total - 1)
        hits = tiles == tile_ids
        return jnp.sum(jnp.where(hits, band_tiles[None, :], 0), axis=1, keepdims=True) * TILE

    proj = jnp.dot(
        embeddings, jnp.concatenate([w_row, w_col], axis=1), preferred_element_type=jnp.float32
    ).astype(jnp.bfloat16)
    gathered = lax.all_gather(proj, "bins", axis=0, tiled=True).astype(jnp.float32)
    row_table = jnp.pad(gathered[:, :MAPS], ((REACH, REACH), (0, 0)))
    row_here = lax.dynamic_slice_in_dim(row_table, row_start, rows + 2 * REACH, 0)
    row_mid = row_here[REACH : REACH + rows].reshape(BLOCKS, SUB, MAPS)
    row_mid = row_mid.transpose(1, 0, 2).reshape(SUB, LANES)
    row_side = jnp.concatenate([row_here[:SUB]] * 2 + [row_here[REACH + rows :]] * 2, axis=1)
    front = band_cols + 2 * REACH
    col_table = jnp.pad(gathered[:, MAPS:], ((front, 4 * REACH), (0, 0)))
    col_here = lax.dynamic_slice_in_dim(
        col_table, row_start - col_start - 192 + front, 384, 0
    )[::-1]
    col_mid = jnp.concatenate([col_here[128 - SUB * q : 352 - SUB * q] for q in range(4)], axis=1)
    col_side = jnp.concatenate([col_here[160:384]] * 2 + [col_here[0:224]] * 2, axis=1)
    taps = conv_w.reshape(LAYERS, 3, 3, MAPS, MAPS)
    same = jnp.eye(BLOCKS, dtype=conv_w.dtype)

    def spread(t):
        full = t[:, :, :, None, :, None, :] * same[:, None, :, None]
        return full.reshape(LAYERS, 3, 3 * LANES, LANES)

    forward = spread(taps.transpose(0, 1, 2, 4, 3))
    backward = spread(taps[:, ::-1, ::-1])
    scales = jnp.sum(choose[None, :, None] * coef, axis=1)
    params = jnp.concatenate([scales, w_out[None], jnp.zeros((5, MAPS), jnp.float32)], axis=0)
    params = jnp.tile(params, (1, BLOCKS))
    goal = jnp.broadcast_to(
        target.reshape(BLOCKS, SUB, width).transpose(1, 2, 0)[..., None],
        (SUB, width, BLOCKS, MAPS),
    ).reshape(SUB * width, LANES)
    near = (row_start // TILE + jnp.arange(-1, 2, dtype=jnp.int32))[:, None]
    limits = jnp.sum(jnp.where(near == tile_ids, band_tiles[None, :], 0), axis=1) * TILE
    kern, stats, row_out, col_out = step_call(
        dilation, limits, col_mid, col_side, row_mid, row_side, forward, backward, params, goal
    )
    kern = kern.reshape(LAYERS, 3, BLOCKS, MAPS, 3, BLOCKS, MAPS)
    kern = sum(kern[:, :, q, :, :, q, :] for q in range(BLOCKS))
    kernels = kern.transpose(0, 1, 3, 2, 4).reshape(LAYERS, 9, MAPS, MAPS)
    stats = jnp.sum(stats, axis=1).reshape(4, BLOCKS, MAPS)
    loss_part = 0.5 * jnp.sum(stats[3, :, 0])
    stats = jnp.sum(stats, axis=1)
    out_grad = stats[2]
    coef_terms = choose[None, :, None] * stats[:2, None, :]
    row_terms = row_out.reshape(SUB, BLOCKS, MAPS).transpose(1, 0, 2).reshape(rows, MAPS)
    col_terms = sum(
        jnp.pad(
            col_out[:, q * MAPS : (q + 1) * MAPS], ((96 - SUB * q, SUB * q), (0, 0))
        )
        for q in range(BLOCKS)
    )[::-1]
    table_base = row_start - col_start - TILE + band_cols
    column_full = jnp.zeros((total_bins + band_cols, MAPS), jnp.float32)
    column_full = lax.dynamic_update_slice(column_full, col_terms, (table_base, zero))
    row_full = jnp.zeros((total_bins, MAPS), jnp.float32)
    row_full = lax.dynamic_update_slice(row_full, row_terms, (row_start, zero))
    both = jnp.concatenate([row_full, column_full[band_cols:]], axis=0).reshape(-1)
    both = all_sum(both, 1).reshape(2, total_bins, MAPS)
    row_total = lax.dynamic_slice_in_dim(both[0], row_start, rows, 0)
    column_total = lax.dynamic_slice_in_dim(both[1], row_start, rows, 0)
    row_all = row_total.astype(jnp.bfloat16)
    column_all = column_total.astype(jnp.bfloat16)
    grad_embeddings = jnp.dot(row_all, w_row.T, preferred_element_type=jnp.float32) + jnp.dot(
        column_all, w_col.T, preferred_element_type=jnp.float32
    )
    share_rows = rows // diag_count
    share_start = lax.axis_index("diag") * share_rows
    row_grad = lax.dynamic_slice_in_dim(row_all, share_start, share_rows, 0)
    col_grad = lax.dynamic_slice_in_dim(column_all, share_start, share_rows, 0)
    piece_rows = lax.dynamic_slice_in_dim(embeddings, share_start, share_rows, 0)
    row_weight = jnp.dot(piece_rows.T, row_grad, preferred_element_type=jnp.float32)
    col_weight = jnp.dot(piece_rows.T, col_grad, preferred_element_type=jnp.float32)
    pieces = (
        kernels,
        row_weight,
        col_weight,
        coef_terms,
        out_grad,
        loss_part.reshape(1),
    )
    flat = all_sum(jnp.concatenate([p.reshape(-1) for p in pieces]), 2)
    sums = []
    at = 0
    for piece in pieces:
        sums.append(flat[at : at + piece.size].reshape(piece.shape))
        at += piece.size
    totals = (sums[5][0], sums[4], sums[0], sums[3], sums[1], sums[2])
    all_bins = jnp.arange(total_bins, dtype=jnp.int32)[:, None]
    count = jnp.sum(jnp.minimum(row_limit(all_bins)[:, 0], all_bins[:, 0] + 1)).astype(jnp.float32)
    inv_root = 1.0 / jnp.sqrt(count)
    loss = jnp.reshape(totals[0] / count, (1,))
    return (
        loss,
        grad_embeddings,
        totals[2] * inv_root,
        totals[3] * inv_root,
        totals[1] * inv_root,
        totals[4] * inv_root,
        totals[5] * inv_root,
    )


def solution(mesh):
    in_specs = (P("bins", None), P(), P(), P(), P(), P(), P(), P(), P(), P("bins", "diag"))
    out_specs = (P(), P("bins", None), P(), P(), P(), P(), P())
    return jax.shard_map(local, mesh=mesh, in_specs=in_specs, out_specs=out_specs, check_vma=False)
```

profile of v0, /device:TPU:0, one launch (start us, length us, event | category | flops | bytes accessed | tf_op | source)
XLA Modules:
  0.0 204.1 jit_solution(7476941701490066300)
XLA Ops:
  0.7 0.9 select_reduce_fusion.1
  1.5 0.5 broadcast_multiply_fusion.3.refs_1_
  2.1 0.9 convolution_convert_fusion
  3.1 15.9 %all_gather.3 = bf16[1024,64]{1,0:T(8,128)(2,1)S(1)} all-gather(bf16[128,64]{1,0:T(8,128)(2,1)S(1)} %bitcast.50), channel_id=1, replica_groups=mesh['bins'=8,'diag'=4] {'bins'}, dimensions={0}, use_global_device_ids=true | all-gather | bytes 147456 | tf_op jit(solution)/shard_map/all_gather | solution.py:533
  21.1 0.9 pad_maximum_fusion.1
  22.1 0.7 reshape.173.refs_4_
  22.8 0.7 pad_maximum_fusion.3.refs_5_
  23.5 1.1 mul.131
  24.6 1.2 mul.132
  26.4 1.1 mul.125
  27.6 1.9 mul.126
  29.5 2.2 %broadcast_multiply_fusion = (bf16[2,3,384,128]{3,2,1,0:T(8,128)(2,1)}, bf16[2,3,384,128]{3,2,1,0:T(8,128)(2,1)}) fusion(bf16[2,3,384,128]{3,2,1,0:T(8,128)(2,1)S(1)} %mul.132, bf16[384,128]{1,0:T(8,128)(2,1)S(1)} %mul.128, bf16[2,3,384,128]{3,2,1,0:T(8,128)(2,1)} %mul.126), kind=kLoop, calls=%fused_computation.16 | loop fusion | flops 589824 | bytes 2457600 | tf_op jit(solution)/shard_map/mul | solution.py:550
  31.7 0.6 fusion.17
  32.3 0.6 compare_convert_fusion
  33.2 0.7 tile.10.refs_8_
  34.2 1.6 copy.119
  35.8 1.9 copy.87.refs_9_
  37.7 99.6 %shard_map.153 = (f32[2,3,128,384]{3,2,1,0:T(8,128)}, f32[4,8,128]{2,1,0:T(8,128)}, f32[32,128]{1,0:T(8,128)}, f32[160,128]{1,0:T(8,128)}) custom-call(s32[2]{0:T(128)} %refs_0_.1, s32[3]{0:T(128)} %broadcast_multiply_fusion.3.refs_1_, f32[224,128]{1,0:T(8,128)} %get-tuple-element.81.refs_2_, f32[224,128]{1,0:T(8,128)} %get-tuple-element.82.refs_3_, ...), custom_call_target="tpu_custom_call" | custom-call | tf_op jit(solution)/shard_map/pallas_call | solution.py:475
  137.3 4.8 %reshape.177 = f32[2,3,4,32,3,4,32]{6,5,4,3,2,1,0:T(4,128)} reshape(f32[2,3,128,384]{3,2,1,0:T(8,128)} %get-tuple-element.11) | data formatting | bytes 2359296 | tf_op jit(solution)/shard_map/reshape | solution.py:567
  142.1 3.6 %fusion.19 = (f32[2,3,1,32,3,1,32]{6,5,4,3,2,1,0:T(1,128)S(1)}, f32[2,3,1,32,3,1,32]{6,5,4,3,2,1,0:T(1,128)S(1)}, f32[2,3,1,32,3,1,32]{6,5,4,3,2,1,0:T(1,128)S(1)}, f32[2,3,1,32,3,1,32]{6,5,4,3,2,1,0:T(1,128)S(1)}) fusion(f32[2,3,4,32,3,4,32]{6,5,4,3,2,1,0:T(4,128)} %reshape.177), kind=kLoop, calls=%fused_computation.70 | loop fusion | bytes 589824 | tf_op jit(solution)/shard_map/slice | solution.py:568
  147.6 25.8 %shard_map.154 = f32[512,128]{1,0:T(8,128)S(1)} custom-call(f32[512,128]{1,0:T(8,128)S(1)} %reshape.180.refs_0_), custom_call_target="tpu_custom_call" | custom-call | tf_op jit(solution)/shard_map/pallas_call | solution.py:100
  174.7 0.6 slice_reduce_fusion
  176.0 0.5 concatenate.27
  176.5 19.0 %shard_map.155 = f32[512,128]{1,0:T(8,128)S(1)} custom-call(f32[512,128]{1,0:T(8,128)S(1)} %pad_bitcast_fusion.refs_0_), custom_call_target="tpu_custom_call" | custom-call | tf_op jit(solution)/shard_map/pallas_call | solution.py:100
  195.5 0.6 slice.172
  196.2 0.6 minimum_reduce_fusion
  198.3 0.9 convolution_add_fusion
  199.2 0.8 mul.143
  200.1 0.7 mul.146
  200.8 0.5 slice_multiply_fusion.4
  201.4 0.7 copy.98
  202.3 0.7 copy.99
  (90 shorter events, 6.8 us)
Async XLA Ops:
  0.6 1.4 copy-start
  19.2 4.4 %copy-start.2 = (bf16[2,9,32,32]{3,2,1,0:T(8,128)(2,1)S(1)}, bf16[2,9,32,32]{3,2,1,0:T(8,128)(2,1)}, u32[]{:S(2)}) copy-start(bf16[2,9,32,32]{3,2,1,0:T(8,128)(2,1)} %param.13) | copy-start | bytes 110596
  27.5 4.2 %copy-start.11 = (s32[4]{0:T(128)S(1)}, s32[4]{0:T(128)}, u32[]{:S(2)}) copy-start(s32[4]{0:T(128)} %param.18) | copy-start | bytes 52
  27.5 5.5 %copy-start.8 = (f32[2,8,32]{2,1,0:T(8,128)S(1)}, f32[2,8,32]{2,1,0:T(8,128)}, u32[]{:S(2)}) copy-start(f32[2,8,32]{2,1,0:T(8,128)} %param.14) | copy-start | bytes 6148
  27.5 5.6 %copy-start.9 = (f32[32]{0:T(128)S(1)}, f32[32]{0:T(128)}, u32[]{:S(2)}) copy-start(f32[32]{0:T(128)} %param.15) | copy-start | bytes 388
  27.5 6.4 %copy-start.5 = (f32[128,128]{1,0:T(8,128)S(1)}, f32[128,128]{1,0:T(8,128)}, u32[]{:S(2)}) copy-start(f32[128,128]{1,0:T(8,128)} %param.19) | copy-start | bytes 196612
  142.1 3.9 %copy-start.1 = (f32[160,128]{1,0:T(8,128)S(1)}, f32[160,128]{1,0:T(8,128)}, u32[]{:S(2)}) copy-start(f32[160,128]{1,0:T(8,128)} %get-tuple-element.13) | copy-start | bytes 245764
  145.7 0.8 copy-start.6
  147.3 27.2 %copy-start.7 = (f32[4,8,128]{2,1,0:T(8,128)S(1)}, f32[4,8,128]{2,1,0:T(8,128)}, u32[]{:S(2)}) copy-start(f32[4,8,128]{2,1,0:T(8,128)} %get-tuple-element.14) | copy-start | bytes 49156
  147.6 48.6 %copy-start.10 = (s32[8]{0:T(128)S(1)}, s32[8]{0:T(128)}, u32[]{:S(2)}) copy-start(s32[8]{0:T(128)} %param.17) | copy-start | bytes 100
  147.6 50.6 %copy-start.3 = (bf16[512,32]{0,1:T(8,128)(2,1)S(1)}, bf16[512,32]{0,1:T(8,128)(2,1)}, u32[]{:S(2)}) copy-start(bf16[512,32]{0,1:T(8,128)(2,1)} %param.11) | copy-start | bytes 98308
  147.6 50.7 %copy-start.4 = (bf16[512,32]{0,1:T(8,128)(2,1)S(1)}, bf16[512,32]{0,1:T(8,128)(2,1)}, u32[]{:S(2)}) copy-start(bf16[512,32]{0,1:T(8,128)(2,1)} %param.12) | copy-start | bytes 98308
where the time goes:
time: 205 us; the launch traced here: 204 us
  Pallas kernels  144 us (70%)
  local copies, waits for them, and re-layouts  28.4 us (14%)
  blocking collectives  15.9 us (8%)
  other arithmetic  8.75 us (4%)
  between operations  4.37 us (2%)
  matrix products  2.37 us (1%)
    pallas_call x1, Pallas kernels, step_call(): pl.pallas_call(lambda *refs: step_kernel(nb, nd, *refs), out_shape=(jax.S...  99.6 us
    pallas_call x2, Pallas kernels, all_sum(): pl.pallas_call(lambda *refs: reduce_kernel(nb, nd, *refs), out_shape=jax....  44.8 us
    all_gather x1, blocking collectives, local(): lax.all_gather(proj, 'bins', axis=0, tiled=True).astype(jnp.float32)  15.9 us
    mul x6, local copies, waits for them, and re-layouts, spread(): full = t[:, :, :, None, :, None, :] * same[:, None, :, None]  5.72 us
    reshape x1, local copies, waits for them, and re-layouts, local(): kern = kern.reshape(LAYERS, 3, BLOCKS, MAPS, 3, BLOCKS, MAPS)  4.82 us

commit v1 on v0

--- a/solution.py
+++ b/solution.py
@@ -123,6 +123,121 @@
     return out.reshape(-1)[: flat.shape[0]]
 
 
+def greet(nb, nd, over_diag):
+    b = lax.axis_index("bins")
+    g = lax.axis_index("diag")
+    barrier = pltpu.get_barrier_semaphore()
+    for k in range(1, nb):
+        pl.semaphore_signal(
+            barrier, inc=1, device_id=(lax.rem(b + k, nb), g), device_id_type=MESH
+        )
+    if over_diag:
+        for k in range(1, nd):
+            pl.semaphore_signal(
+                barrier, inc=1, device_id=(b, lax.rem(g + k, nd)), device_id_type=MESH
+            )
+    pl.semaphore_wait(barrier, nb - 1 + (nd - 1 if over_diag else 0))
+
+
+def send_to(src, dst, ssem, rsem, target):
+    copy = pltpu.make_async_remote_copy(
+        src_ref=src,
+        dst_ref=dst,
+        send_sem=ssem,
+        recv_sem=rsem,
+        device_id=target,
+        device_id_type=MESH,
+    )
+    copy.start()
+    return copy
+
+
+def gather_kernel(nb, nd, x_ref, o_ref, ssem, rsem):
+    b = lax.axis_index("bins")
+    g = lax.axis_index("diag")
+    greet(nb, nd, False)
+    rows = x_ref.shape[0]
+    mine = pl.ds(pl.multiple_of(b * rows, rows), rows)
+    copies = [
+        send_to(x_ref, o_ref.at[mine], ssem.at[k], rsem.at[k], (lax.rem(b + k, nb), g))
+        for k in range(1, nb)
+    ]
+    o_ref[mine, :] = x_ref[...]
+    for copy in copies:
+        copy.wait()
+
+
+def gather_bins(x):
+    nb, nd = lax.axis_size("bins"), lax.axis_size("diag")
+    vmem = pl.BlockSpec(memory_space=pltpu.VMEM)
+    return pl.pallas_call(
+        lambda *refs: gather_kernel(nb, nd, *refs),
+        out_shape=jax.ShapeDtypeStruct((nb * x.shape[0], x.shape[1]), x.dtype),
+        in_specs=[vmem],
+        out_specs=vmem,
+        scratch_shapes=[pltpu.SemaphoreType.DMA((nb,)), pltpu.SemaphoreType.DMA((nb,))],
+        compiler_params=pltpu.CompilerParams(
+            collective_id=4, has_side_effects=True, vmem_limit_bytes=8 * 2**20
+        ),
+    )(x)
+
+
+def owner_kernel(nb, nd, row_ref, col_ref, o_ref, buf_b, buf_g, sb, rb, sg, rg):
+    b = lax.axis_index("bins")
+    g = lax.axis_index("diag")
+    greet(nb, nd, True)
+    rows = row_ref.shape[0]
+
+    def rows_of(index):
+        return pl.ds(pl.multiple_of(index * rows, 8), rows)
+
+    peers = [lax.rem(b + k, nb) for k in range(nb)]
+    copies = [
+        send_to(col_ref.at[rows_of(peers[k])], buf_b.at[k], sb.at[k], rb.at[k], (peers[k], g))
+        for k in range(1, nb)
+    ]
+    total = col_ref[rows_of(b), :]
+    for k in range(1, nb):
+        copies[k - 1].wait()
+        total = total + buf_b[k]
+    buf_g[g, 0:rows, :] = row_ref[...]
+    buf_g[g, rows : 2 * rows, :] = total
+    copies = [
+        send_to(buf_g.at[g], buf_g.at[g], sg.at[k], rg.at[k], (b, lax.rem(g + k, nd)))
+        for k in range(1, nd)
+    ]
+    for copy in copies:
+        copy.wait()
+    total = buf_g[0]
+    for k in range(1, nd):
+        total = total + buf_g[k]
+    o_ref[...] = total
+
+
+def owner_sum(row, col):
+    nb, nd = lax.axis_size("bins"), lax.axis_size("diag")
+    vmem = pl.BlockSpec(memory_space=pltpu.VMEM)
+    dma = pltpu.SemaphoreType.DMA
+    rows = row.shape[0]
+    return pl.pallas_call(
+        lambda *refs: owner_kernel(nb, nd, *refs),
+        out_shape=jax.ShapeDtypeStruct((2 * rows, 128), jnp.float32),
+        in_specs=[vmem, vmem],
+        out_specs=vmem,
+        scratch_shapes=[
+            pltpu.VMEM((nb, rows, 128), jnp.float32),
+            pltpu.VMEM((nd, 2 * rows, 128), jnp.float32),
+            dma((nb,)),
+            dma((nb,)),
+            dma((nd,)),
+            dma((nd,)),
+        ],
+        compiler_params=pltpu.CompilerParams(
+            collective_id=1, has_side_effects=True, vmem_limit_bytes=8 * 2**20
+        ),
+    )(row, col)
+
+
 DIRS = [(-1, 0), (1, 0), (0, -1), (0, 1), (-1, -1), (-1, 1), (1, -1), (1, 1)]
 BLOCKS = 4
 SUB = 32
@@ -528,16 +643,18 @@
         return jnp.sum(jnp.where(hits, band_tiles[None, :], 0), axis=1, keepdims=True) * TILE
 
     proj = jnp.dot(
-        embeddings, jnp.concatenate([w_row, w_col], axis=1), preferred_element_type=jnp.float32
+        embeddings,
+        jnp.pad(jnp.concatenate([w_row, w_col], axis=1), ((0, 0), (0, LANES - 2 * MAPS))),
+        preferred_element_type=jnp.float32
     ).astype(jnp.bfloat16)
-    gathered = lax.all_gather(proj, "bins", axis=0, tiled=True).astype(jnp.float32)
+    gathered = gather_bins(proj).astype(jnp.float32)
     row_table = jnp.pad(gathered[:, :MAPS], ((REACH, REACH), (0, 0)))
     row_here = lax.dynamic_slice_in_dim(row_table, row_start, rows + 2 * REACH, 0)
     row_mid = row_here[REACH : REACH + rows].reshape(BLOCKS, SUB, MAPS)
     row_mid = row_mid.transpose(1, 0, 2).reshape(SUB, LANES)
     row_side = jnp.concatenate([row_here[:SUB]] * 2 + [row_here[REACH + rows :]] * 2, axis=1)
     front = band_cols + 2 * REACH
-    col_table = jnp.pad(gathered[:, MAPS:], ((front, 4 * REACH), (0, 0)))
+    col_table = jnp.pad(gathered[:, MAPS : 2 * MAPS], ((front, 4 * REACH), (0, 0)))
     col_here = lax.dynamic_slice_in_dim(
         col_table, row_start - col_start - 192 + front, 384, 0
     )[::-1]
@@ -582,12 +699,8 @@
     table_base = row_start - col_start - TILE + band_cols
     column_full = jnp.zeros((total_bins + band_cols, MAPS), jnp.float32)
     column_full = lax.dynamic_update_slice(column_full, col_terms, (table_base, zero))
-    row_full = jnp.zeros((total_bins, MAPS), jnp.float32)
-    row_full = lax.dynamic_update_slice(row_full, row_terms, (row_start, zero))
-    both = jnp.concatenate([row_full, column_full[band_cols:]], axis=0).reshape(-1)
-    both = all_sum(both, 1).reshape(2, total_bins, MAPS)
-    row_total = lax.dynamic_slice_in_dim(both[0], row_start, rows, 0)
-    column_total = lax.dynamic_slice_in_dim(both[1], row_start, rows, 0)
+    both = owner_sum(row_terms.reshape(-1, 128), column_full[band_cols:].reshape(-1, 128))
+    row_total, column_total = both.reshape(2, rows, MAPS)
     row_all = row_total.astype(jnp.bfloat16)
     column_all = column_total.astype(jnp.bfloat16)
     grad_embeddings = jnp.dot(row_all, w_row.T, preferred_element_type=jnp.float32) + jnp.dot(

time: 205 us -> 189 us (0.922)
  blocking collectives: 15.9 us -> 0 us
    pallas_call x0 -> x2, Pallas kernels: none -> 26 us  [the longest x1 15.7 us: owner_sum(): pl.pallas_call(lambda *refs: owner_kernel(nb, nd, *refs), out_shape=jax.S...]
    pallas_call x2 -> x1, Pallas kernels: 44.8 us -> 20.8 us  [all_sum(): pl.pallas_call(lambda *refs: reduce_kernel(nb, nd, *refs), out_shape=jax....]
    all_gather x1 -> x0, blocking collectives: 15.9 us -> none  [local(): lax.all_gather(proj, 'bins', axis=0, tiled=True).astype(jnp.float32)]
where the time goes in v1:
time: 189 us; the launch traced here: 188 us
  Pallas kernels  146 us (77%)
  local copies, waits for them, and re-layouts  27.3 us (14%)
  other arithmetic  8.74 us (5%)
  between operations  4.31 us (2%)
  matrix products  2.38 us (1%)
    pallas_call x1, Pallas kernels, step_call(): pl.pallas_call(lambda *refs: step_kernel(nb, nd, *refs), out_shape=(jax.S...  99 us
    pallas_call x1, Pallas kernels, all_sum(): pl.pallas_call(lambda *refs: reduce_kernel(nb, nd, *refs), out_shape=jax....  20.8 us
    pallas_call x1, Pallas kernels, owner_sum(): pl.pallas_call(lambda *refs: owner_kernel(nb, nd, *refs), out_shape=jax.S...  15.7 us
    pallas_call x1, Pallas kernels, gather_bins(): pl.pallas_call(lambda *refs: gather_kernel(nb, nd, *refs), out_shape=jax....  10.2 us
    mul x6, local copies, waits for them, and re-layouts, spread(): full = t[:, :, :, None, :, None, :] * same[:, None, :, None]  5.72 us
    reshape x1, local copies, waits for them, and re-layouts, local(): kern = kern.reshape(LAYERS, 3, BLOCKS, MAPS, 3, BLOCKS, MAPS)  4.82 us

profile of v1, /device:TPU:0, one launch (start us, length us, event | category | flops | bytes accessed | tf_op | source)
XLA Modules:
  0.0 188.5 jit_solution(9149432679308501667)
XLA Ops:
  0.7 0.9 select_reduce_fusion.1
  1.5 0.5 broadcast_multiply_fusion.3.refs_1_
  2.1 0.9 fusion.refs_0_
  3.0 10.2 %shard_map.153 = bf16[1024,128]{1,0:T(8,128)(2,1)S(1)} custom-call(bf16[128,128]{1,0:T(8,128)(2,1)S(1)} %fusion.refs_0_), custom_call_target="tpu_custom_call" | custom-call | tf_op jit(solution)/shard_map/pallas_call | solution.py:173
  15.3 0.9 pad_maximum_fusion
  16.4 0.7 reshape.171.refs_4_
  17.1 0.7 pad_maximum_fusion.2.refs_5_
  17.8 1.1 mul.131
  18.9 1.2 mul.132
  20.7 1.1 mul.125
  21.8 1.9 %mul.126 = bf16[2,3,384,128]{3,2,1,0:T(8,128)(2,1)} reshape(bf16[2,3,3,4,32,4,32]{6,5,4,3,2,1,0:T(4,128)(2,1)S(1)} %mul.125) | data formatting | bytes 1179648 | tf_op jit(solution)/shard_map/mul | solution.py:667
  23.7 2.2 %broadcast_multiply_fusion = (bf16[2,3,384,128]{3,2,1,0:T(8,128)(2,1)}, bf16[2,3,384,128]{3,2,1,0:T(8,128)(2,1)}) fusion(bf16[2,3,384,128]{3,2,1,0:T(8,128)(2,1)S(1)} %mul.132, bf16[384,128]{1,0:T(8,128)(2,1)S(1)} %mul.128, bf16[2,3,384,128]{3,2,1,0:T(8,128)(2,1)} %mul.126), kind=kLoop, calls=%fused_computation.17 | loop fusion | flops 589824 | bytes 2457600 | tf_op jit(solution)/shard_map/mul | solution.py:667
  26.0 0.6 fusion.24
  26.6 0.6 compare_convert_fusion
  27.5 0.7 tile.10.refs_8_
  28.4 1.6 copy.86
  30.1 1.9 copy.54.refs_9_
  31.9 99.0 %shard_map.154 = (f32[2,3,128,384]{3,2,1,0:T(8,128)}, f32[4,8,128]{2,1,0:T(8,128)}, f32[32,128]{1,0:T(8,128)}, f32[160,128]{1,0:T(8,128)}) custom-call(s32[2]{0:T(128)} %refs_0_.1, s32[3]{0:T(128)} %broadcast_multiply_fusion.3.refs_1_, f32[224,128]{1,0:T(8,128)} %get-tuple-element.67.refs_2_, f32[224,128]{1,0:T(8,128)} %get-tuple-element.68.refs_3_, ...), custom_call_target="tpu_custom_call" | custom-call | tf_op jit(solution)/shard_map/pallas_call | solution.py:590
  130.9 4.8 %reshape.175 = f32[2,3,4,32,3,4,32]{6,5,4,3,2,1,0:T(4,128)} reshape(f32[2,3,128,384]{3,2,1,0:T(8,128)} %get-tuple-element.11) | data formatting | bytes 2359296 | tf_op jit(solution)/shard_map/reshape | solution.py:684
  135.8 3.6 %fusion.28 = (f32[2,3,1,32,3,1,32]{6,5,4,3,2,1,0:T(1,128)S(1)}, f32[2,3,1,32,3,1,32]{6,5,4,3,2,1,0:T(1,128)S(1)}, f32[2,3,1,32,3,1,32]{6,5,4,3,2,1,0:T(1,128)S(1)}, f32[2,3,1,32,3,1,32]{6,5,4,3,2,1,0:T(1,128)S(1)}) fusion(f32[2,3,4,32,3,4,32]{6,5,4,3,2,1,0:T(4,128)} %reshape.175), kind=kLoop, calls=%fused_computation.75 | loop fusion | bytes 589824 | tf_op jit(solution)/shard_map/slice | solution.py:685
  140.4 15.7 %shard_map.155 = f32[64,128]{1,0:T(8,128)S(1)} custom-call(f32[32,128]{1,0:T(8,128)S(1)} %reshape_reshape.7.refs_0_, f32[256,128]{1,0:T(8,128)S(1)} %reshape.177.refs_1_), custom_call_target="tpu_custom_call" | custom-call | tf_op jit(solution)/shard_map/pallas_call | solution.py:222
  157.3 0.6 slice_reduce_fusion
  158.6 0.5 concatenate.23
  159.1 20.8 %shard_map.156 = f32[512,128]{1,0:T(8,128)S(1)} custom-call(f32[512,128]{1,0:T(8,128)S(1)} %pad_bitcast_fusion.refs_0_), custom_call_target="tpu_custom_call" | custom-call | tf_op jit(solution)/shard_map/pallas_call | solution.py:100
  179.8 0.6 slice.166
  180.5 0.6 minimum_reduce_fusion
  182.6 0.9 convolution_add_fusion
  183.5 0.8 mul.143
  184.4 0.7 mul.146
  185.1 0.5 slice_multiply_fusion.4
  185.7 0.7 copy.63
  186.6 0.7 copy.64
  (83 shorter events, 5.7 us)
Async XLA Ops:
  0.6 1.4 copy-start
  13.4 4.4 %copy-start.2 = (bf16[2,9,32,32]{3,2,1,0:T(8,128)(2,1)S(1)}, bf16[2,9,32,32]{3,2,1,0:T(8,128)(2,1)}, u32[]{:S(2)}) copy-start(bf16[2,9,32,32]{3,2,1,0:T(8,128)(2,1)} %param.13) | copy-start | bytes 110596
  21.8 4.2 %copy-start.11 = (s32[4]{0:T(128)S(1)}, s32[4]{0:T(128)}, u32[]{:S(2)}) copy-start(s32[4]{0:T(128)} %param.18) | copy-start | bytes 52
  21.8 5.5 %copy-start.8 = (f32[2,8,32]{2,1,0:T(8,128)S(1)}, f32[2,8,32]{2,1,0:T(8,128)}, u32[]{:S(2)}) copy-start(f32[2,8,32]{2,1,0:T(8,128)} %param.14) | copy-start | bytes 6148
  21.8 5.6 %copy-start.9 = (f32[32]{0:T(128)S(1)}, f32[32]{0:T(128)}, u32[]{:S(2)}) copy-start(f32[32]{0:T(128)} %param.15) | copy-start | bytes 388
  21.8 6.4 %copy-start.3 = (f32[128,128]{1,0:T(8,128)S(1)}, f32[128,128]{1,0:T(8,128)}, u32[]{:S(2)}) copy-start(f32[128,128]{1,0:T(8,128)} %param.19) | copy-start | bytes 196612
  135.8 3.8 %copy-start.6 = (f32[32,128]{1,0:T(8,128)S(1)}, f32[32,128]{1,0:T(8,128)}, u32[]{:S(2)}) copy-start(f32[32,128]{1,0:T(8,128)} %get-tuple-element.12) | copy-start | bytes 49156
  135.8 4.0 %copy-start.1 = (f32[160,128]{1,0:T(8,128)S(1)}, f32[160,128]{1,0:T(8,128)}, u32[]{:S(2)}) copy-start(f32[160,128]{1,0:T(8,128)} %get-tuple-element.13) | copy-start | bytes 245764
  140.0 17.0 %copy-start.7 = (f32[4,8,128]{2,1,0:T(8,128)S(1)}, f32[4,8,128]{2,1,0:T(8,128)}, u32[]{:S(2)}) copy-start(f32[4,8,128]{2,1,0:T(8,128)} %get-tuple-element.14) | copy-start | bytes 49156
  140.2 40.3 %copy-start.10 = (s32[8]{0:T(128)S(1)}, s32[8]{0:T(128)}, u32[]{:S(2)}) copy-start(s32[8]{0:T(128)} %param.17) | copy-start | bytes 100
  140.2 42.3 %copy-start.4 = (bf16[512,32]{0,1:T(8,128)(2,1)S(1)}, bf16[512,32]{0,1:T(8,128)(2,1)}, u32[]{:S(2)}) copy-start(bf16[512,32]{0,1:T(8,128)(2,1)} %param.11) | copy-start | bytes 98308
  140.2 42.4 %copy-start.5 = (bf16[512,32]{0,1:T(8,128)(2,1)S(1)}, bf16[512,32]{0,1:T(8,128)(2,1)}, u32[]{:S(2)}) copy-start(bf16[512,32]{0,1:T(8,128)(2,1)} %param.12) | copy-start | bytes 98308
